TPU v7x, 32 devices: a whole 2x2x4 slice. The times are simulated.
32 devices in a mesh: horiz: 8 (over z, y), vert: 4 (over x, core).
Axes of the slice: x: 2, y: 2, z: 4, core: 2. Of those that a mesh axis runs over, the one named last changes fastest.
Arguments:
- tracer: bfloat16 [8, 2048, 128], P('vert', 'horiz'), may hold values from -6 to 6
- explicit_tiles: bfloat16 [8, 16, 7, 128, 128], P('vert', 'horiz'), may hold values from -0.25 to 0.25
- tile_columns: int32 [8, 16, 7], P('vert', 'horiz'), may hold values from 0 to 127, as said below
- tile_counts: int32 [8, 16], P('vert', 'horiz'), may hold values from 4 to 7
- surface_source: bfloat16 [2048, 128], P('horiz'), may hold values from -6 to 6
- implicit_columns: float32 [2048, 8, 8], P(('horiz', 'vert')), may hold values from -0.53033009 to 1
- settling: float32 [128], replicated, may hold values from 0.02 to 0.5
- wet_mask: int32 [8, 2048], P('vert', 'horiz'), may hold values 0 or 1
Outputs:
- tracer_out: bfloat16 [8, 2048, 128], P('vert', 'horiz')
Inputs may be any that keep to these rules, and one draw needn't show every extreme that they name: `tile_columns`: slot 0 of block row (l, t) names the row's own tile l * 16 + t; the other slots name distinct tiles within 2 levels and 2 tiles of it, inside the grid.
All inputs are finite; a program needn't handle non-finite values. No bound on the sum of `wet_mask` on one device may be relied on, other than what follows from the above.
Results may differ from a plain program's by a relative error of at most 0.015.
Values may be sent and summed in bfloat16 or wider, within the bound.
A program may use at most 64 MiB of HBM per device.

v0:
```python
import jax
import jax.numpy as jnp
from jax import lax
from jax.sharding import PartitionSpec as P

REACH = 2
STEPS = 4


def extended(shard, sides, width):
    for axis, dim in sides:
        size, length = (lax.axis_size(axis), shard.shape[dim])
        up = [(i, (i + 1) % size) for i in range(size - 1)]
        down = [(j, i) for i, j in up]
        last = lax.slice_in_dim(shard, length - width, length, axis=dim)
        leading = lax.slice_in_dim(shard, 0, width, axis=dim)
        before = lax.ppermute(last, axis, up)
        after = lax.ppermute(leading, axis, down)
        shard = jnp.concatenate([before, shard, after], axis=dim)
    return shard


def from_behind(value, axis, steps):
    count = lax.axis_size(axis)
    leading, last = (max(0, -steps), min(count, count - steps))
    return lax.ppermute(value, axis, [(source, source + steps) for source in range(leading, last)])


def on_device(
    tracer,
    explicit_tiles,
    tile_columns,
    tile_counts,
    surface_source,
    implicit_columns,
    settling,
    wet_mask,
):
    lev_dev, cells_dev, classes = tracer.shape
    tile_size = explicit_tiles.shape[-1]
    tiles_dev = cells_dev // tile_size
    slot_count = explicit_tiles.shape[2]
    h_tiles = tiles_dev * lax.axis_size("horiz")
    wide_tiles = tiles_dev + 2 * REACH
    first_level = lax.axis_index("vert") * lev_dev
    first_tile = lax.axis_index("horiz") * tiles_dev
    col_level = tile_columns // h_tiles - (first_level - REACH)
    col_tile = tile_columns % h_tiles - (first_tile - REACH)
    position = col_level * wide_tiles + col_tile
    live_slots = (
        jnp.arange(slot_count, dtype=jnp.int32)[None, None, :] < tile_counts[:, :, None]
    ).astype(jnp.bfloat16)
    on_top = first_level + jnp.arange(lev_dev, dtype=jnp.int32) == 0
    source = surface_source.astype(jnp.float32)
    fall_rate = settling[None, None, :]
    wet_cells = wet_mask.astype(jnp.bfloat16)[:, :, None]
    all_columns = lax.all_gather(implicit_columns, "vert", axis=0, tiled=True)
    own_rows = lax.dynamic_slice_in_dim(all_columns, first_level, lev_dev, 1)
    current = tracer
    for step_index in range(STEPS):
        slab_grid = current.reshape(lev_dev, tiles_dev, tile_size, classes)
        padded = extended(slab_grid, (("horiz", 1), ("vert", 0)), REACH)
        flattened = padded.reshape(-1, tile_size, classes)
        picked = flattened[position] * live_slots[:, :, :, None, None]
        explicit_flow = jnp.einsum(
            "ltjab,ltjbs->ltas", explicit_tiles, picked, preferred_element_type=jnp.float32
        )
        explicit_flow = explicit_flow.reshape(lev_dev, cells_dev, classes)
        explicit_flow = explicit_flow + jnp.where(on_top[:, None, None], source[None, :, :], 0.0)
        loaded = explicit_flow.astype(jnp.bfloat16)
        mixed_col = jnp.einsum(
            "ckm,mcs->kcs",
            own_rows,
            lax.all_gather(loaded, "vert", axis=0, tiled=True).astype(jnp.float32),
            precision=lax.Precision.HIGHEST,
        )
        upper_level = from_behind(mixed_col[-1].astype(jnp.bfloat16), "vert", 1).astype(jnp.float32)
        from_above = jnp.concatenate([upper_level[None], mixed_col[:-1]], axis=0)
        settled = (1.0 - fall_rate) * mixed_col + fall_rate * from_above
        current = (settled * wet_cells.astype(jnp.float32)).astype(jnp.bfloat16)
    return current


def solution(mesh):
    placed = (
        P("vert", "horiz", None),
        P("vert", "horiz", None, None, None),
        P("vert", "horiz", None),
        P("vert", "horiz"),
        P("horiz", None),
        P(("horiz", "vert"), None, None),
        P(),
        P("vert", "horiz"),
    )
    return jax.shard_map(
        on_device, mesh=mesh, in_specs=placed, out_specs=P("vert", "horiz", None), check_vma=False
    )
```

profile of v0, /device:TPU:1, one launch (start us, length us, event | category | flops | bytes accessed | tf_op | source)
XLA Modules:
  0.0 167.6 jit_solution(6005104641196930024)
XLA Ops:
  0.0 1.4 collective-permute-start.1
  1.4 4.6 %collective-permute-start = (bf16[2,2,128,128]{3,2,1,0:T(8,128)(2,1)}, bf16[2,2,128,128]{3,2,1,0:T(8,128)(2,1)S(1)}, u32[]{:S(2)}, u32[]{:S(2)}) collective-permute-start(bf16[2,2,128,128]{3,2,1,0:T(8,128)(2,1)} %bitcast.83), channel_id=1, source_target_pairs={{0,4},{4,8},{8,12},{12,16},{16,20},{20,24},{24,28},{1,5},{5,9},{9,... | collective-permute-start | bytes 393224 | tf_op jit(solution)/shard_map/ppermute | solution.py:17
  8.7 11.3 %all_gather.16 = f32[256,8,8]{2,1,0:T(8,128)S(1)} all-gather(f32[64,8,8]{2,1,0:T(8,128)S(1)} %copy.38), channel_id=1, replica_groups=mesh['horiz'=8,'vert'=4] {'vert'}, dimensions={0}, use_global_device_ids=true | all-gather | bytes 81920 | tf_op jit(solution)/shard_map/all_gather | solution.py:57
  20.1 2.1 %collective-permute-start.3 = (bf16[2,6,128,128]{3,2,1,0:T(8,128)(2,1)S(1)}, bf16[2,6,128,128]{3,2,1,0:T(8,128)(2,1)S(1)}, u32[]{:S(2)}, u32[]{:S(2)}) collective-permute-start(bf16[2,6,128,128]{3,2,1,0:T(8,128)(2,1)S(1)} %pad_maximum_fusion.4), channel_id=1, source_target_pairs={{1,0},{2,1},{3,2},{5,4},{6,5},{7,6},{9,8},{10,9},{11,10},{13,12},{... | collective-permute-start | bytes 1179656 | tf_op jit(solution)/shard_map/ppermute | solution.py:18
  22.1 3.5 %collective-permute-start.2 = (bf16[2,6,128,128]{3,2,1,0:T(8,128)(2,1)S(1)}, bf16[2,6,128,128]{3,2,1,0:T(8,128)(2,1)S(1)}, u32[]{:S(2)}, u32[]{:S(2)}) collective-permute-start(bf16[2,6,128,128]{3,2,1,0:T(8,128)(2,1)S(1)} %pad_maximum_fusion.4), channel_id=1, source_target_pairs={{0,1},{1,2},{2,3},{4,5},{5,6},{6,7},{8,9},{9,10},{10,11},{12,13},{... | collective-permute-start | bytes 1179656 | tf_op jit(solution)/shard_map/ppermute | solution.py:17
  25.7 3.4 %collective-permute-done.3 = bf16[2,6,128,128]{3,2,1,0:T(8,128)(2,1)S(1)} collective-permute-done((bf16[2,6,128,128]{3,2,1,0:T(8,128)(2,1)S(1)}, bf16[2,6,128,128]{3,2,1,0:T(8,128)(2,1)S(1)}, u32[]{:S(2)}, u32[]{:S(2)}) %collective-permute-start.3) | collective-permute-done | bytes 393248 | tf_op jit(solution)/shard_map/ppermute | solution.py:18
  31.4 1.6 gather_fusion
  33.0 1.7 fusion.6
  34.8 8.4 %all_gather.15 = bf16[8,256,128]{2,1,0:T(8,128)(2,1)S(1)} all-gather(bf16[2,256,128]{2,1,0:T(8,128)(2,1)S(1)} %fusion.16), channel_id=1, replica_groups=mesh['horiz'=8,'vert'=4] {'vert'}, dimensions={0}, use_global_device_ids=true | all-gather | bytes 655360 | tf_op jit(solution)/shard_map/all_gather | solution.py:74
  44.6 2.5 %collective-permute-start.4 = (bf16[256,128]{1,0:T(8,128)(2,1)S(1)}, bf16[256,128]{1,0:T(8,128)(2,1)S(1)}, u32[]{:S(2)}, u32[]{:S(2)}) collective-permute-start(bf16[256,128]{1,0:T(8,128)(2,1)S(1)} %bitcast.90), channel_id=1, source_target_pairs={{0,1},{1,2},{2,3},{4,5},{5,6},{6,7},{8,9},{9,10},{10,11},{12,13},{... | collective-permute-start | bytes 196616 | tf_op jit(solution)/shard_map/ppermute | solution.py:26
  48.8 4.0 %collective-permute-start.5 = (bf16[2,2,128,128]{3,2,1,0:T(8,128)(2,1)S(1)}, bf16[2,2,128,128]{3,2,1,0:T(8,128)(2,1)S(1)}, u32[]{:S(2)}, u32[]{:S(2)}) collective-permute-start(bf16[2,2,128,128]{3,2,1,0:T(8,128)(2,1)S(1)} %copy.42), channel_id=1, source_target_pairs={{0,4},{4,8},{8,12},{12,16},{16,20},{20,24},{24,28},{1,5},{5,9},{9,... | collective-permute-start | bytes 393224 | tf_op jit(solution)/shard_map/ppermute | solution.py:17
  52.9 1.3 collective-permute-start.6
  54.2 2.0 %collective-permute-done.5 = bf16[2,2,128,128]{3,2,1,0:T(8,128)(2,1)S(1)} collective-permute-done((bf16[2,2,128,128]{3,2,1,0:T(8,128)(2,1)S(1)}, bf16[2,2,128,128]{3,2,1,0:T(8,128)(2,1)S(1)}, u32[]{:S(2)}, u32[]{:S(2)}) %collective-permute-start.5) | collective-permute-done | bytes 131104 | tf_op jit(solution)/shard_map/ppermute | solution.py:17
  56.2 3.8 %collective-permute-done.6 = bf16[2,2,128,128]{3,2,1,0:T(8,128)(2,1)S(1)} collective-permute-done((bf16[2,2,128,128]{3,2,1,0:T(8,128)(2,1)S(1)}, bf16[2,2,128,128]{3,2,1,0:T(8,128)(2,1)S(1)}, u32[]{:S(2)}, u32[]{:S(2)}) %collective-permute-start.6) | collective-permute-done | bytes 131104 | tf_op jit(solution)/shard_map/ppermute | solution.py:18
  60.1 2.5 %collective-permute-start.8 = (bf16[2,6,128,128]{3,2,1,0:T(8,128)(2,1)S(1)}, bf16[2,6,128,128]{3,2,1,0:T(8,128)(2,1)S(1)}, u32[]{:S(2)}, u32[]{:S(2)}) collective-permute-start(bf16[2,6,128,128]{3,2,1,0:T(8,128)(2,1)S(1)} %constant_dynamic-update-slice_fusion), channel_id=1, source_target_pairs={{1,0},{2,1},{3,2},{5,4},{6,5},{7,6},{9,8},{10,9},{11,10},{13,12},{... | collective-permute-start | bytes 1179656 | tf_op jit(solution)/shard_map/ppermute | solution.py:18
  62.6 3.6 %collective-permute-start.7 = (bf16[2,6,128,128]{3,2,1,0:T(8,128)(2,1)S(1)}, bf16[2,6,128,128]{3,2,1,0:T(8,128)(2,1)S(1)}, u32[]{:S(2)}, u32[]{:S(2)}) collective-permute-start(bf16[2,6,128,128]{3,2,1,0:T(8,128)(2,1)S(1)} %constant_dynamic-update-slice_fusion), channel_id=1, source_target_pairs={{0,1},{1,2},{2,3},{4,5},{5,6},{6,7},{8,9},{9,10},{10,11},{12,13},{... | collective-permute-start | bytes 1179656 | tf_op jit(solution)/shard_map/ppermute | solution.py:17
  66.2 3.5 %collective-permute-done.8 = bf16[2,6,128,128]{3,2,1,0:T(8,128)(2,1)S(1)} collective-permute-done((bf16[2,6,128,128]{3,2,1,0:T(8,128)(2,1)S(1)}, bf16[2,6,128,128]{3,2,1,0:T(8,128)(2,1)S(1)}, u32[]{:S(2)}, u32[]{:S(2)}) %collective-permute-start.8) | collective-permute-done | bytes 393248 | tf_op jit(solution)/shard_map/ppermute | solution.py:18
  71.1 1.6 gather_fusion.1
  72.7 1.6 fusion.4
  74.5 8.4 %all_gather.17 = bf16[8,256,128]{2,1,0:T(8,128)(2,1)S(1)} all-gather(bf16[2,256,128]{2,1,0:T(8,128)(2,1)S(1)} %fusion.17), channel_id=1, replica_groups=mesh['horiz'=8,'vert'=4] {'vert'}, dimensions={0}, use_global_device_ids=true | all-gather | bytes 655360 | tf_op jit(solution)/shard_map/all_gather | solution.py:74
  84.2 2.5 %collective-permute-start.9 = (bf16[256,128]{1,0:T(8,128)(2,1)S(1)}, bf16[256,128]{1,0:T(8,128)(2,1)S(1)}, u32[]{:S(2)}, u32[]{:S(2)}) collective-permute-start(bf16[256,128]{1,0:T(8,128)(2,1)S(1)} %bitcast.91), channel_id=1, source_target_pairs={{0,1},{1,2},{2,3},{4,5},{5,6},{6,7},{8,9},{9,10},{10,11},{12,13},{... | collective-permute-start | bytes 196616 | tf_op jit(solution)/shard_map/ppermute | solution.py:26
  86.8 1.2 collective-permute-done.9
  88.5 3.1 %collective-permute-start.10 = (bf16[2,2,128,128]{3,2,1,0:T(8,128)(2,1)S(1)}, bf16[2,2,128,128]{3,2,1,0:T(8,128)(2,1)S(1)}, u32[]{:S(2)}, u32[]{:S(2)}) collective-permute-start(bf16[2,2,128,128]{3,2,1,0:T(8,128)(2,1)S(1)} %copy.47), channel_id=1, source_target_pairs={{0,4},{4,8},{8,12},{12,16},{16,20},{20,24},{24,28},{1,5},{5,9},{9,... | collective-permute-start | bytes 393224 | tf_op jit(solution)/shard_map/ppermute | solution.py:17
  91.6 1.3 collective-permute-start.11
  92.9 2.0 %collective-permute-done.10 = bf16[2,2,128,128]{3,2,1,0:T(8,128)(2,1)S(1)} collective-permute-done((bf16[2,2,128,128]{3,2,1,0:T(8,128)(2,1)S(1)}, bf16[2,2,128,128]{3,2,1,0:T(8,128)(2,1)S(1)}, u32[]{:S(2)}, u32[]{:S(2)}) %collective-permute-start.10) | collective-permute-done | bytes 131104 | tf_op jit(solution)/shard_map/ppermute | solution.py:17
  95.0 3.8 %collective-permute-done.11 = bf16[2,2,128,128]{3,2,1,0:T(8,128)(2,1)S(1)} collective-permute-done((bf16[2,2,128,128]{3,2,1,0:T(8,128)(2,1)S(1)}, bf16[2,2,128,128]{3,2,1,0:T(8,128)(2,1)S(1)}, u32[]{:S(2)}, u32[]{:S(2)}) %collective-permute-start.11) | collective-permute-done | bytes 131104 | tf_op jit(solution)/shard_map/ppermute | solution.py:18
  98.8 2.5 %collective-permute-start.13 = (bf16[2,6,128,128]{3,2,1,0:T(8,128)(2,1)S(1)}, bf16[2,6,128,128]{3,2,1,0:T(8,128)(2,1)S(1)}, u32[]{:S(2)}, u32[]{:S(2)}) collective-permute-start(bf16[2,6,128,128]{3,2,1,0:T(8,128)(2,1)S(1)} %constant_dynamic-update-slice_fusion.3), channel_id=1, source_target_pairs={{1,0},{2,1},{3,2},{5,4},{6,5},{7,6},{9,8},{10,9},{11,10},{13,12},{... | collective-permute-start | bytes 1179656 | tf_op jit(solution)/shard_map/ppermute | solution.py:18
  101.4 3.6 %collective-permute-start.12 = (bf16[2,6,128,128]{3,2,1,0:T(8,128)(2,1)S(1)}, bf16[2,6,128,128]{3,2,1,0:T(8,128)(2,1)S(1)}, u32[]{:S(2)}, u32[]{:S(2)}) collective-permute-start(bf16[2,6,128,128]{3,2,1,0:T(8,128)(2,1)S(1)} %constant_dynamic-update-slice_fusion.3), channel_id=1, source_target_pairs={{0,1},{1,2},{2,3},{4,5},{5,6},{6,7},{8,9},{9,10},{10,11},{12,13},{... | collective-permute-start | bytes 1179656 | tf_op jit(solution)/shard_map/ppermute | solution.py:17
  105.0 3.5 %collective-permute-done.13 = bf16[2,6,128,128]{3,2,1,0:T(8,128)(2,1)S(1)} collective-permute-done((bf16[2,6,128,128]{3,2,1,0:T(8,128)(2,1)S(1)}, bf16[2,6,128,128]{3,2,1,0:T(8,128)(2,1)S(1)}, u32[]{:S(2)}, u32[]{:S(2)}) %collective-permute-start.13) | collective-permute-done | bytes 393248 | tf_op jit(solution)/shard_map/ppermute | solution.py:18
  109.8 1.6 gather_fusion.2
  111.5 1.7 fusion.2
  113.2 8.4 %all_gather.18 = bf16[8,256,128]{2,1,0:T(8,128)(2,1)S(1)} all-gather(bf16[2,256,128]{2,1,0:T(8,128)(2,1)S(1)} %fusion.18), channel_id=1, replica_groups=mesh['horiz'=8,'vert'=4] {'vert'}, dimensions={0}, use_global_device_ids=true | all-gather | bytes 655360 | tf_op jit(solution)/shard_map/all_gather | solution.py:74
  121.6 1.2 convolution_bitcast_fusion.1
  123.0 2.5 %collective-permute-start.14 = (bf16[256,128]{1,0:T(8,128)(2,1)S(1)}, bf16[256,128]{1,0:T(8,128)(2,1)S(1)}, u32[]{:S(2)}, u32[]{:S(2)}) collective-permute-start(bf16[256,128]{1,0:T(8,128)(2,1)S(1)} %bitcast.92), channel_id=1, source_target_pairs={{0,1},{1,2},{2,3},{4,5},{5,6},{6,7},{8,9},{9,10},{10,11},{12,13},{... | collective-permute-start | bytes 196616 | tf_op jit(solution)/shard_map/ppermute | solution.py:26
  125.6 1.2 collective-permute-done.14
  127.2 4.1 %collective-permute-start.15 = (bf16[2,2,128,128]{3,2,1,0:T(8,128)(2,1)S(1)}, bf16[2,2,128,128]{3,2,1,0:T(8,128)(2,1)S(1)}, u32[]{:S(2)}, u32[]{:S(2)}) collective-permute-start(bf16[2,2,128,128]{3,2,1,0:T(8,128)(2,1)S(1)} %copy.51), channel_id=1, source_target_pairs={{0,4},{4,8},{8,12},{12,16},{16,20},{20,24},{24,28},{1,5},{5,9},{9,... | collective-permute-start | bytes 393224 | tf_op jit(solution)/shard_map/ppermute | solution.py:17
  131.3 1.3 collective-permute-start.16
  132.6 2.0 %collective-permute-done.15 = bf16[2,2,128,128]{3,2,1,0:T(8,128)(2,1)S(1)} collective-permute-done((bf16[2,2,128,128]{3,2,1,0:T(8,128)(2,1)S(1)}, bf16[2,2,128,128]{3,2,1,0:T(8,128)(2,1)S(1)}, u32[]{:S(2)}, u32[]{:S(2)}) %collective-permute-start.15) | collective-permute-done | bytes 131104 | tf_op jit(solution)/shard_map/ppermute | solution.py:17
  134.6 3.8 %collective-permute-done.16 = bf16[2,2,128,128]{3,2,1,0:T(8,128)(2,1)S(1)} collective-permute-done((bf16[2,2,128,128]{3,2,1,0:T(8,128)(2,1)S(1)}, bf16[2,2,128,128]{3,2,1,0:T(8,128)(2,1)S(1)}, u32[]{:S(2)}, u32[]{:S(2)}) %collective-permute-start.16) | collective-permute-done | bytes 131104 | tf_op jit(solution)/shard_map/ppermute | solution.py:18
  138.5 2.5 %collective-permute-start.18 = (bf16[2,6,128,128]{3,2,1,0:T(8,128)(2,1)S(1)}, bf16[2,6,128,128]{3,2,1,0:T(8,128)(2,1)S(1)}, u32[]{:S(2)}, u32[]{:S(2)}) collective-permute-start(bf16[2,6,128,128]{3,2,1,0:T(8,128)(2,1)S(1)} %constant_dynamic-update-slice_fusion.6), channel_id=1, source_target_pairs={{1,0},{2,1},{3,2},{5,4},{6,5},{7,6},{9,8},{10,9},{11,10},{13,12},{... | collective-permute-start | bytes 1179656 | tf_op jit(solution)/shard_map/ppermute | solution.py:18
  141.0 3.8 %collective-permute-start.17 = (bf16[2,6,128,128]{3,2,1,0:T(8,128)(2,1)S(1)}, bf16[2,6,128,128]{3,2,1,0:T(8,128)(2,1)S(1)}, u32[]{:S(2)}, u32[]{:S(2)}) collective-permute-start(bf16[2,6,128,128]{3,2,1,0:T(8,128)(2,1)S(1)} %constant_dynamic-update-slice_fusion.6), channel_id=1, source_target_pairs={{0,1},{1,2},{2,3},{4,5},{5,6},{6,7},{8,9},{9,10},{10,11},{12,13},{... | collective-permute-start | bytes 1179656 | tf_op jit(solution)/shard_map/ppermute | solution.py:17
  144.9 3.3 %collective-permute-done.18 = bf16[2,6,128,128]{3,2,1,0:T(8,128)(2,1)S(1)} collective-permute-done((bf16[2,6,128,128]{3,2,1,0:T(8,128)(2,1)S(1)}, bf16[2,6,128,128]{3,2,1,0:T(8,128)(2,1)S(1)}, u32[]{:S(2)}, u32[]{:S(2)}) %collective-permute-start.18) | collective-permute-done | bytes 393248 | tf_op jit(solution)/shard_map/ppermute | solution.py:18
  149.5 1.6 gather_fusion.3
  151.1 1.6 fusion
  152.9 8.4 %all_gather.19 = bf16[8,256,128]{2,1,0:T(8,128)(2,1)S(1)} all-gather(bf16[2,256,128]{2,1,0:T(8,128)(2,1)S(1)} %fusion.19), channel_id=1, replica_groups=mesh['horiz'=8,'vert'=4] {'vert'}, dimensions={0}, use_global_device_ids=true | all-gather | bytes 655360 | tf_op jit(solution)/shard_map/all_gather | solution.py:74
  161.3 1.2 convolution_bitcast_fusion
  162.7 2.5 %collective-permute-start.19 = (bf16[256,128]{1,0:T(8,128)(2,1)S(1)}, bf16[256,128]{1,0:T(8,128)(2,1)S(1)}, u32[]{:S(2)}, u32[]{:S(2)}) collective-permute-start(bf16[256,128]{1,0:T(8,128)(2,1)S(1)} %bitcast.93), channel_id=1, source_target_pairs={{0,1},{1,2},{2,3},{4,5},{5,6},{6,7},{8,9},{9,10},{10,11},{12,13},{... | collective-permute-start | bytes 196616 | tf_op jit(solution)/shard_map/ppermute | solution.py:26
  165.3 1.2 collective-permute-done.19
  (73 shorter events, 16.3 us)
Async XLA Ops:
  0.0 33.0 %copy-start = (bf16[2,2,7,128,128]{4,3,2,1,0:T(8,128)(2,1)S(1)}, bf16[2,2,7,128,128]{4,3,2,1,0:T(8,128)(2,1)}, u32[]{:S(2)}) copy-start(bf16[2,2,7,128,128]{4,3,2,1,0:T(8,128)(2,1)} %param.9) | copy-start | bytes 2752516
  0.0 20.0 %copy-start.1 = (bf16[2,256,128]{2,1,0:T(8,128)(2,1)S(1)}, bf16[2,256,128]{2,1,0:T(8,128)(2,1)}, u32[]{:S(2)}) copy-start(bf16[2,256,128]{2,1,0:T(8,128)(2,1)} %param.8) | copy-start | bytes 393220
  0.0 20.0 %collective-permute-start.1 = (bf16[2,2,128,128]{3,2,1,0:T(8,128)(2,1)}, bf16[2,2,128,128]{3,2,1,0:T(8,128)(2,1)S(1)}, u32[]{:S(2)}, u32[]{:S(2)}) collective-permute-start(bf16[2,2,128,128]{3,2,1,0:T(8,128)(2,1)} %bitcast.82), channel_id=1, source_target_pairs={{4,0},{8,4},{12,8},{16,12},{20,16},{24,20},{28,24},{5,1},{9,5},{13... | collective-permute-start | bytes 393224 | tf_op jit(solution)/shard_map/ppermute | solution.py:18
  1.4 18.6 %collective-permute-start = (bf16[2,2,128,128]{3,2,1,0:T(8,128)(2,1)}, bf16[2,2,128,128]{3,2,1,0:T(8,128)(2,1)S(1)}, u32[]{:S(2)}, u32[]{:S(2)}) collective-permute-start(bf16[2,2,128,128]{3,2,1,0:T(8,128)(2,1)} %bitcast.83), channel_id=1, source_target_pairs={{0,4},{4,8},{8,12},{12,16},{16,20},{20,24},{24,28},{1,5},{5,9},{9,... | collective-permute-start | bytes 393224 | tf_op jit(solution)/shard_map/ppermute | solution.py:17
  7.7 17.9 %copy-start.5 = (s32[2,2]{1,0:T(2,128)S(1)}, s32[2,2]{1,0:T(2,128)}, u32[]{:S(2)}) copy-start(s32[2,2]{1,0:T(2,128)} %param.11) | copy-start | bytes 52
  7.7 18.0 %copy-start.4 = (s32[2,256]{1,0:T(2,128)S(1)}, s32[2,256]{1,0:T(2,128)}, u32[]{:S(2)}) copy-start(s32[2,256]{1,0:T(2,128)} %param.15) | copy-start | bytes 6148
  20.0 9.2 %copy-start.2 = (bf16[2,2,128,128]{3,2,1,0:T(8,128)(2,1)}, bf16[2,2,128,128]{3,2,1,0:T(8,128)(2,1)S(1)}, u32[]{:S(2)}) copy-start(bf16[2,2,128,128]{3,2,1,0:T(8,128)(2,1)S(1)} %collective-permute-done) | copy-start | bytes 393220
  20.1 9.1 %collective-permute-start.3 = (bf16[2,6,128,128]{3,2,1,0:T(8,128)(2,1)S(1)}, bf16[2,6,128,128]{3,2,1,0:T(8,128)(2,1)S(1)}, u32[]{:S(2)}, u32[]{:S(2)}) collective-permute-start(bf16[2,6,128,128]{3,2,1,0:T(8,128)(2,1)S(1)} %pad_maximum_fusion.4), channel_id=1, source_target_pairs={{1,0},{2,1},{3,2},{5,4},{6,5},{7,6},{9,8},{10,9},{11,10},{13,12},{... | collective-permute-start | bytes 1179656 | tf_op jit(solution)/shard_map/ppermute | solution.py:18
  22.1 8.2 %collective-permute-start.2 = (bf16[2,6,128,128]{3,2,1,0:T(8,128)(2,1)S(1)}, bf16[2,6,128,128]{3,2,1,0:T(8,128)(2,1)S(1)}, u32[]{:S(2)}, u32[]{:S(2)}) collective-permute-start(bf16[2,6,128,128]{3,2,1,0:T(8,128)(2,1)S(1)} %pad_maximum_fusion.4), channel_id=1, source_target_pairs={{0,1},{1,2},{2,3},{4,5},{5,6},{6,7},{8,9},{9,10},{10,11},{12,13},{... | collective-permute-start | bytes 1179656 | tf_op jit(solution)/shard_map/ppermute | solution.py:17
  34.8 12.3 %copy-start.3 = (f32[128]{0:T(128)S(1)}, f32[128]{0:T(128)}, u32[]{:S(2)}) copy-start(f32[128]{0:T(128)} %param.14) | copy-start | bytes 1540
  44.6 3.8 %collective-permute-start.4 = (bf16[256,128]{1,0:T(8,128)(2,1)S(1)}, bf16[256,128]{1,0:T(8,128)(2,1)S(1)}, u32[]{:S(2)}, u32[]{:S(2)}) collective-permute-start(bf16[256,128]{1,0:T(8,128)(2,1)S(1)} %bitcast.90), channel_id=1, source_target_pairs={{0,1},{1,2},{2,3},{4,5},{5,6},{6,7},{8,9},{9,10},{10,11},{12,13},{... | collective-permute-start | bytes 196616 | tf_op jit(solution)/shard_map/ppermute | solution.py:26
  48.8 7.3 %collective-permute-start.5 = (bf16[2,2,128,128]{3,2,1,0:T(8,128)(2,1)S(1)}, bf16[2,2,128,128]{3,2,1,0:T(8,128)(2,1)S(1)}, u32[]{:S(2)}, u32[]{:S(2)}) collective-permute-start(bf16[2,2,128,128]{3,2,1,0:T(8,128)(2,1)S(1)} %copy.42), channel_id=1, source_target_pairs={{0,4},{4,8},{8,12},{12,16},{16,20},{20,24},{24,28},{1,5},{5,9},{9,... | collective-permute-start | bytes 393224 | tf_op jit(solution)/shard_map/ppermute | solution.py:17
  52.9 7.2 %collective-permute-start.6 = (bf16[2,2,128,128]{3,2,1,0:T(8,128)(2,1)S(1)}, bf16[2,2,128,128]{3,2,1,0:T(8,128)(2,1)S(1)}, u32[]{:S(2)}, u32[]{:S(2)}) collective-permute-start(bf16[2,2,128,128]{3,2,1,0:T(8,128)(2,1)S(1)} %copy.42), channel_id=1, source_target_pairs={{4,0},{8,4},{12,8},{16,12},{20,16},{24,20},{28,24},{5,1},{9,5},{13... | collective-permute-start | bytes 393224 | tf_op jit(solution)/shard_map/ppermute | solution.py:18
  60.1 9.7 %collective-permute-start.8 = (bf16[2,6,128,128]{3,2,1,0:T(8,128)(2,1)S(1)}, bf16[2,6,128,128]{3,2,1,0:T(8,128)(2,1)S(1)}, u32[]{:S(2)}, u32[]{:S(2)}) collective-permute-start(bf16[2,6,128,128]{3,2,1,0:T(8,128)(2,1)S(1)} %constant_dynamic-update-slice_fusion), channel_id=1, source_target_pairs={{1,0},{2,1},{3,2},{5,4},{6,5},{7,6},{9,8},{10,9},{11,10},{13,12},{... | collective-permute-start | bytes 1179656 | tf_op jit(solution)/shard_map/ppermute | solution.py:18
  62.6 8.3 %collective-permute-start.7 = (bf16[2,6,128,128]{3,2,1,0:T(8,128)(2,1)S(1)}, bf16[2,6,128,128]{3,2,1,0:T(8,128)(2,1)S(1)}, u32[]{:S(2)}, u32[]{:S(2)}) collective-permute-start(bf16[2,6,128,128]{3,2,1,0:T(8,128)(2,1)S(1)} %constant_dynamic-update-slice_fusion), channel_id=1, source_target_pairs={{0,1},{1,2},{2,3},{4,5},{5,6},{6,7},{8,9},{9,10},{10,11},{12,13},{... | collective-permute-start | bytes 1179656 | tf_op jit(solution)/shard_map/ppermute | solution.py:17
  84.2 3.8 %collective-permute-start.9 = (bf16[256,128]{1,0:T(8,128)(2,1)S(1)}, bf16[256,128]{1,0:T(8,128)(2,1)S(1)}, u32[]{:S(2)}, u32[]{:S(2)}) collective-permute-start(bf16[256,128]{1,0:T(8,128)(2,1)S(1)} %bitcast.91), channel_id=1, source_target_pairs={{0,1},{1,2},{2,3},{4,5},{5,6},{6,7},{8,9},{9,10},{10,11},{12,13},{... | collective-permute-start | bytes 196616 | tf_op jit(solution)/shard_map/ppermute | solution.py:26
  88.5 6.4 %collective-permute-start.10 = (bf16[2,2,128,128]{3,2,1,0:T(8,128)(2,1)S(1)}, bf16[2,2,128,128]{3,2,1,0:T(8,128)(2,1)S(1)}, u32[]{:S(2)}, u32[]{:S(2)}) collective-permute-start(bf16[2,2,128,128]{3,2,1,0:T(8,128)(2,1)S(1)} %copy.47), channel_id=1, source_target_pairs={{0,4},{4,8},{8,12},{12,16},{16,20},{20,24},{24,28},{1,5},{5,9},{9,... | collective-permute-start | bytes 393224 | tf_op jit(solution)/shard_map/ppermute | solution.py:17
  91.6 7.2 %collective-permute-start.11 = (bf16[2,2,128,128]{3,2,1,0:T(8,128)(2,1)S(1)}, bf16[2,2,128,128]{3,2,1,0:T(8,128)(2,1)S(1)}, u32[]{:S(2)}, u32[]{:S(2)}) collective-permute-start(bf16[2,2,128,128]{3,2,1,0:T(8,128)(2,1)S(1)} %copy.47), channel_id=1, source_target_pairs={{4,0},{8,4},{12,8},{16,12},{20,16},{24,20},{28,24},{5,1},{9,5},{13... | collective-permute-start | bytes 393224 | tf_op jit(solution)/shard_map/ppermute | solution.py:18
  98.8 9.7 %collective-permute-start.13 = (bf16[2,6,128,128]{3,2,1,0:T(8,128)(2,1)S(1)}, bf16[2,6,128,128]{3,2,1,0:T(8,128)(2,1)S(1)}, u32[]{:S(2)}, u32[]{:S(2)}) collective-permute-start(bf16[2,6,128,128]{3,2,1,0:T(8,128)(2,1)S(1)} %constant_dynamic-update-slice_fusion.3), channel_id=1, source_target_pairs={{1,0},{2,1},{3,2},{5,4},{6,5},{7,6},{9,8},{10,9},{11,10},{13,12},{... | collective-permute-start | bytes 1179656 | tf_op jit(solution)/shard_map/ppermute | solution.py:18
  101.4 8.3 %collective-permute-start.12 = (bf16[2,6,128,128]{3,2,1,0:T(8,128)(2,1)S(1)}, bf16[2,6,128,128]{3,2,1,0:T(8,128)(2,1)S(1)}, u32[]{:S(2)}, u32[]{:S(2)}) collective-permute-start(bf16[2,6,128,128]{3,2,1,0:T(8,128)(2,1)S(1)} %constant_dynamic-update-slice_fusion.3), channel_id=1, source_target_pairs={{0,1},{1,2},{2,3},{4,5},{5,6},{6,7},{8,9},{9,10},{10,11},{12,13},{... | collective-permute-start | bytes 1179656 | tf_op jit(solution)/shard_map/ppermute | solution.py:17
  123.0 3.8 %collective-permute-start.14 = (bf16[256,128]{1,0:T(8,128)(2,1)S(1)}, bf16[256,128]{1,0:T(8,128)(2,1)S(1)}, u32[]{:S(2)}, u32[]{:S(2)}) collective-permute-start(bf16[256,128]{1,0:T(8,128)(2,1)S(1)} %bitcast.92), channel_id=1, source_target_pairs={{0,1},{1,2},{2,3},{4,5},{5,6},{6,7},{8,9},{9,10},{10,11},{12,13},{... | collective-permute-start | bytes 196616 | tf_op jit(solution)/shard_map/ppermute | solution.py:26
  127.2 7.3 %collective-permute-start.15 = (bf16[2,2,128,128]{3,2,1,0:T(8,128)(2,1)S(1)}, bf16[2,2,128,128]{3,2,1,0:T(8,128)(2,1)S(1)}, u32[]{:S(2)}, u32[]{:S(2)}) collective-permute-start(bf16[2,2,128,128]{3,2,1,0:T(8,128)(2,1)S(1)} %copy.51), channel_id=1, source_target_pairs={{0,4},{4,8},{8,12},{12,16},{16,20},{20,24},{24,28},{1,5},{5,9},{9,... | collective-permute-start | bytes 393224 | tf_op jit(solution)/shard_map/ppermute | solution.py:17
  131.3 7.2 %collective-permute-start.16 = (bf16[2,2,128,128]{3,2,1,0:T(8,128)(2,1)S(1)}, bf16[2,2,128,128]{3,2,1,0:T(8,128)(2,1)S(1)}, u32[]{:S(2)}, u32[]{:S(2)}) collective-permute-start(bf16[2,2,128,128]{3,2,1,0:T(8,128)(2,1)S(1)} %copy.51), channel_id=1, source_target_pairs={{4,0},{8,4},{12,8},{16,12},{20,16},{24,20},{28,24},{5,1},{9,5},{13... | collective-permute-start | bytes 393224 | tf_op jit(solution)/shard_map/ppermute | solution.py:18
  138.5 9.7 %collective-permute-start.18 = (bf16[2,6,128,128]{3,2,1,0:T(8,128)(2,1)S(1)}, bf16[2,6,128,128]{3,2,1,0:T(8,128)(2,1)S(1)}, u32[]{:S(2)}, u32[]{:S(2)}) collective-permute-start(bf16[2,6,128,128]{3,2,1,0:T(8,128)(2,1)S(1)} %constant_dynamic-update-slice_fusion.6), channel_id=1, source_target_pairs={{1,0},{2,1},{3,2},{5,4},{6,5},{7,6},{9,8},{10,9},{11,10},{13,12},{... | collective-permute-start | bytes 1179656 | tf_op jit(solution)/shard_map/ppermute | solution.py:18
  141.0 8.3 %collective-permute-start.17 = (bf16[2,6,128,128]{3,2,1,0:T(8,128)(2,1)S(1)}, bf16[2,6,128,128]{3,2,1,0:T(8,128)(2,1)S(1)}, u32[]{:S(2)}, u32[]{:S(2)}) collective-permute-start(bf16[2,6,128,128]{3,2,1,0:T(8,128)(2,1)S(1)} %constant_dynamic-update-slice_fusion.6), channel_id=1, source_target_pairs={{0,1},{1,2},{2,3},{4,5},{5,6},{6,7},{8,9},{9,10},{10,11},{12,13},{... | collective-permute-start | bytes 1179656 | tf_op jit(solution)/shard_map/ppermute | solution.py:17
  162.7 3.8 %collective-permute-start.19 = (bf16[256,128]{1,0:T(8,128)(2,1)S(1)}, bf16[256,128]{1,0:T(8,128)(2,1)S(1)}, u32[]{:S(2)}, u32[]{:S(2)}) collective-permute-start(bf16[256,128]{1,0:T(8,128)(2,1)S(1)} %bitcast.93), channel_id=1, source_target_pairs={{0,1},{1,2},{2,3},{4,5},{5,6},{6,7},{8,9},{9,10},{10,11},{12,13},{... | collective-permute-start | bytes 196616 | tf_op jit(solution)/shard_map/ppermute | solution.py:26
where the time goes:
time: 169 us; the launch traced here: 168 us
  starting transfers between devices  55.3 us (33%)
  blocking collectives  44.9 us (27%)
  waiting for transfers between devices  40.7 us (24%)
  matrix products  11.4 us (7%)
  local copies, waits for them, and re-layouts  9.57 us (6%)
  other arithmetic  5.1 us (3%)
    all_gather x4, blocking collectives, on_device(): lax.all_gather(loaded, 'vert', axis=0, tiled=True).astype(jnp.float32)  33.6 us
    ppermute x8, starting transfers between devices, extended(): before = lax.ppermute(last, axis, up)  30.4 us
    ppermute x8, waiting for transfers between devices, extended(): after = lax.ppermute(leading, axis, down)  25.3 us
    ppermute x8, starting transfers between devices, extended(): after = lax.ppermute(leading, axis, down)  14.9 us
    all_gather x1, blocking collectives, on_device(): all_columns = lax.all_gather(implicit_columns, 'vert', axis=0, tiled=True)  11.3 us
    ppermute x8, waiting for transfers between devices, extended(): before = lax.ppermute(last, axis, up)  10.7 us
    ppermute x4, starting transfers between devices, from_behind(): lax.ppermute(value, axis, [(source, source + steps) for source in range(l...  10 us
    dot_general x4, matrix products, on_device(): jnp.einsum('ltjab,ltjbs->ltas', explicit_tiles, picked, preferred_element...  6.59 us
  transfers between devices with their start and end apart: 20, of which 18 were waited for; matrix products, arithmetic and copies ran while one was open for 2% of the time, Pallas kernels for 0%

commit v1 on v0

--- a/solution.py
+++ b/solution.py
@@ -54,7 +54,15 @@
     source = surface_source.astype(jnp.float32)
     fall_rate = settling[None, None, :]
     wet_cells = wet_mask.astype(jnp.bfloat16)[:, :, None]
-    all_columns = lax.all_gather(implicit_columns, "vert", axis=0, tiled=True)
+    ways, here, step = (lax.axis_size("vert"), lax.axis_index("vert"), implicit_columns.shape[0])
+    line, have = (implicit_columns, 1)
+    while have < ways:
+        line = jnp.concatenate(
+            [line, lax.ppermute(line, "vert", [(d, (d - have) % ways) for d in range(ways)])],
+            axis=0,
+        )
+        have = 2 * have
+    all_columns = jnp.roll(line, here * step, axis=0)
     own_rows = lax.dynamic_slice_in_dim(all_columns, first_level, lev_dev, 1)
     current = tracer
     for step_index in range(STEPS):

time: 169 us -> 157 us (0.929)
  blocking collectives: 44.9 us -> 33 us
  local copies, waits for them, and re-layouts: 9.57 us -> 5.37 us
  other arithmetic: 5.1 us -> 8.29 us
  matrix products: 11.4 us -> 8.65 us
  starting transfers between devices: 55.3 us -> 58 us
    all_gather x1 -> x0, blocking collectives: 11.3 us -> none  [on_device(): all_columns = lax.all_gather(implicit_columns, 'vert', axis=0, tiled=True)]
    ppermute x0 -> x2, waiting for transfers between devices: none -> 3.63 us  [on_device(): lax.ppermute(line, 'vert', [(d, (d - have) % ways) for d in range(ways)])]
    gather x4, local copies, waits for them, and re-layouts: 6.5 us -> 2.89 us  [on_device(): picked = flattened[position] * live_slots[:, :, :, None, None]]
    ppermute x8, waiting for transfers between devices: 25.3 us -> 22.1 us  [extended(): after = lax.ppermute(leading, axis, down)]
    dot_general x4, matrix products: 6.59 us -> 3.92 us  [on_device(): jnp.einsum('ltjab,ltjbs->ltas', explicit_tiles, picked, preferred_element...]
  transfers between devices with their start and end apart: 20 -> 22, of which waited for: 18 -> 18; matrix products, arithmetic and copies ran while one was open for 2% -> 4% of each run, Pallas kernels for 0% -> 0%
where the time goes in v1:
time: 157 us; the launch traced here: 155 us
  starting transfers between devices  58 us (37%)
  waiting for transfers between devices  41 us (26%)
  blocking collectives  33 us (21%)
  matrix products  8.65 us (6%)
  other arithmetic  8.29 us (5%)
  local copies, waits for them, and re-layouts  5.37 us (3%)
    all_gather x4, blocking collectives, on_device(): lax.all_gather(loaded, 'vert', axis=0, tiled=True).astype(jnp.float32)  33 us
    ppermute x8, starting transfers between devices, extended(): before = lax.ppermute(last, axis, up)  31.3 us
    ppermute x8, waiting for transfers between devices, extended(): after = lax.ppermute(leading, axis, down)  22.1 us
    ppermute x8, starting transfers between devices, extended(): after = lax.ppermute(leading, axis, down)  14.7 us
    ppermute x4, starting transfers between devices, from_behind(): lax.ppermute(value, axis, [(source, source + steps) for source in range(l...  10.9 us
    ppermute x8, waiting for transfers between devices, extended(): before = lax.ppermute(last, axis, up)  10.6 us
    dot_general x4, matrix products, on_device(): jnp.einsum('ckm,mcs->kcs', own_rows, lax.all_gather(loaded, 'vert', axis=...  4.73 us
    ppermute x4, waiting for transfers between devices, from_behind(): lax.ppermute(value, axis, [(source, source + steps) for source in range(l...  4.68 us
  transfers between devices with their start and end apart: 22, of which 18 were waited for; matrix products, arithmetic and copies ran while one was open for 4% of the time, Pallas kernels for 0%

profile of v1, /device:TPU:1, one launch (start us, length us, event | category | flops | bytes accessed | tf_op | source)
XLA Modules:
  0.0 154.9 jit_solution(3982645391818163522)
XLA Ops:
  0.0 1.4 collective-permute-start.1
  1.4 4.6 %collective-permute-start = (bf16[2,2,128,128]{3,2,1,0:T(8,128)(2,1)}, bf16[2,2,128,128]{3,2,1,0:T(8,128)(2,1)S(1)}, u32[]{:S(2)}, u32[]{:S(2)}) collective-permute-start(bf16[2,2,128,128]{3,2,1,0:T(8,128)(2,1)} %bitcast.87), channel_id=1, source_target_pairs={{0,4},{4,8},{8,12},{12,16},{16,20},{20,24},{24,28},{1,5},{5,9},{9,... | collective-permute-start | bytes 393224 | tf_op jit(solution)/shard_map/ppermute | solution.py:17
  9.3 2.1 %collective-permute-done = bf16[2,2,128,128]{3,2,1,0:T(8,128)(2,1)S(1)} collective-permute-done((bf16[2,2,128,128]{3,2,1,0:T(8,128)(2,1)}, bf16[2,2,128,128]{3,2,1,0:T(8,128)(2,1)S(1)}, u32[]{:S(2)}, u32[]{:S(2)}) %collective-permute-start) | collective-permute-done | bytes 131104 | tf_op jit(solution)/shard_map/ppermute | solution.py:17
  12.3 2.4 %collective-permute-start.3 = (bf16[2,6,128,128]{3,2,1,0:T(8,128)(2,1)S(1)}, bf16[2,6,128,128]{3,2,1,0:T(8,128)(2,1)S(1)}, u32[]{:S(2)}, u32[]{:S(2)}) collective-permute-start(bf16[2,6,128,128]{3,2,1,0:T(8,128)(2,1)S(1)} %pad_maximum_fusion.4), channel_id=1, source_target_pairs={{1,0},{2,1},{3,2},{5,4},{6,5},{7,6},{9,8},{10,9},{11,10},{13,12},{... | collective-permute-start | bytes 1179656 | tf_op jit(solution)/shard_map/ppermute | solution.py:18
  14.7 3.2 %collective-permute-start.2 = (bf16[2,6,128,128]{3,2,1,0:T(8,128)(2,1)S(1)}, bf16[2,6,128,128]{3,2,1,0:T(8,128)(2,1)}, u32[]{:S(2)}, u32[]{:S(2)}) collective-permute-start(bf16[2,6,128,128]{3,2,1,0:T(8,128)(2,1)S(1)} %pad_maximum_fusion.4), channel_id=1, source_target_pairs={{0,1},{1,2},{2,3},{4,5},{5,6},{6,7},{8,9},{9,10},{10,11},{12,13},{... | collective-permute-start | bytes 1179656 | tf_op jit(solution)/shard_map/ppermute | solution.py:17
  19.7 3.6 %collective-permute-done.5 = f32[128,8,8]{0,2,1:T(8,128)S(1)} collective-permute-done((f32[128,8,8]{0,2,1:T(8,128)S(1)}, f32[128,8,8]{0,2,1:T(8,128)S(1)}, u32[]{:S(2)}, u32[]{:S(2)}) %collective-permute-start.5) | collective-permute-done | bytes 32800 | tf_op jit(solution)/shard_map/ppermute | solution.py:61
  23.7 1.1 pad_maximum_fusion
  26.1 7.8 %all_gather.12 = bf16[8,256,128]{2,1,0:T(8,128)(2,1)S(1)} all-gather(bf16[2,256,128]{2,1,0:T(8,128)(2,1)S(1)} %fusion.16), channel_id=1, replica_groups=mesh['horiz'=8,'vert'=4] {'vert'}, dimensions={0}, use_global_device_ids=true | all-gather | bytes 655360 | tf_op jit(solution)/shard_map/all_gather | solution.py:82
  33.9 1.2 convolution_bitcast_fusion.3
  35.3 3.4 %collective-permute-start.6 = (bf16[256,128]{1,0:T(8,128)(2,1)S(1)}, bf16[256,128]{1,0:T(8,128)(2,1)S(1)}, u32[]{:S(2)}, u32[]{:S(2)}) collective-permute-start(bf16[256,128]{1,0:T(8,128)(2,1)S(1)} %bitcast.94), channel_id=1, source_target_pairs={{0,1},{1,2},{2,3},{4,5},{5,6},{6,7},{8,9},{9,10},{10,11},{12,13},{... | collective-permute-start | bytes 196616 | tf_op jit(solution)/shard_map/ppermute | solution.py:26
  40.4 4.0 %collective-permute-start.7 = (bf16[2,2,128,128]{3,2,1,0:T(8,128)(2,1)S(1)}, bf16[2,2,128,128]{3,2,1,0:T(8,128)(2,1)S(1)}, u32[]{:S(2)}, u32[]{:S(2)}) collective-permute-start(bf16[2,2,128,128]{3,2,1,0:T(8,128)(2,1)S(1)} %copy.48), channel_id=1, source_target_pairs={{0,4},{4,8},{8,12},{12,16},{16,20},{20,24},{24,28},{1,5},{5,9},{9,... | collective-permute-start | bytes 393224 | tf_op jit(solution)/shard_map/ppermute | solution.py:17
  44.5 1.3 collective-permute-start.8
  46.8 4.0 %collective-permute-done.8 = bf16[2,2,128,128]{3,2,1,0:T(8,128)(2,1)S(1)} collective-permute-done((bf16[2,2,128,128]{3,2,1,0:T(8,128)(2,1)S(1)}, bf16[2,2,128,128]{3,2,1,0:T(8,128)(2,1)S(1)}, u32[]{:S(2)}, u32[]{:S(2)}) %collective-permute-start.8) | collective-permute-done | bytes 131104 | tf_op jit(solution)/shard_map/ppermute | solution.py:18
  50.9 2.0 %collective-permute-start.10 = (bf16[2,6,128,128]{3,2,1,0:T(8,128)(2,1)S(1)}, bf16[2,6,128,128]{3,2,1,0:T(8,128)(2,1)S(1)}, u32[]{:S(2)}, u32[]{:S(2)}) collective-permute-start(bf16[2,6,128,128]{3,2,1,0:T(8,128)(2,1)S(1)} %constant_dynamic-update-slice_fusion), channel_id=1, source_target_pairs={{1,0},{2,1},{3,2},{5,4},{6,5},{7,6},{9,8},{10,9},{11,10},{13,12},{... | collective-permute-start | bytes 1179656 | tf_op jit(solution)/shard_map/ppermute | solution.py:18
  52.9 5.0 %collective-permute-start.9 = (bf16[2,6,128,128]{3,2,1,0:T(8,128)(2,1)S(1)}, bf16[2,6,128,128]{3,2,1,0:T(8,128)(2,1)S(1)}, u32[]{:S(2)}, u32[]{:S(2)}) collective-permute-start(bf16[2,6,128,128]{3,2,1,0:T(8,128)(2,1)S(1)} %constant_dynamic-update-slice_fusion), channel_id=1, source_target_pairs={{0,1},{1,2},{2,3},{4,5},{5,6},{6,7},{8,9},{9,10},{10,11},{12,13},{... | collective-permute-start | bytes 1179656 | tf_op jit(solution)/shard_map/ppermute | solution.py:17
  57.8 3.5 %collective-permute-done.10 = bf16[2,6,128,128]{3,2,1,0:T(8,128)(2,1)S(1)} collective-permute-done((bf16[2,6,128,128]{3,2,1,0:T(8,128)(2,1)S(1)}, bf16[2,6,128,128]{3,2,1,0:T(8,128)(2,1)S(1)}, u32[]{:S(2)}, u32[]{:S(2)}) %collective-permute-start.10) | collective-permute-done | bytes 393248 | tf_op jit(solution)/shard_map/ppermute | solution.py:18
  61.3 1.2 collective-permute-done.9
  63.4 1.2 fusion.4
  64.7 8.4 %all_gather.13 = bf16[8,256,128]{2,1,0:T(8,128)(2,1)S(1)} all-gather(bf16[2,256,128]{2,1,0:T(8,128)(2,1)S(1)} %fusion.17), channel_id=1, replica_groups=mesh['horiz'=8,'vert'=4] {'vert'}, dimensions={0}, use_global_device_ids=true | all-gather | bytes 655360 | tf_op jit(solution)/shard_map/all_gather | solution.py:82
  73.0 1.2 convolution_bitcast_fusion.2
  74.4 2.5 %collective-permute-start.11 = (bf16[256,128]{1,0:T(8,128)(2,1)S(1)}, bf16[256,128]{1,0:T(8,128)(2,1)S(1)}, u32[]{:S(2)}, u32[]{:S(2)}) collective-permute-start(bf16[256,128]{1,0:T(8,128)(2,1)S(1)} %bitcast.95), channel_id=1, source_target_pairs={{0,1},{1,2},{2,3},{4,5},{5,6},{6,7},{8,9},{9,10},{10,11},{12,13},{... | collective-permute-start | bytes 196616 | tf_op jit(solution)/shard_map/ppermute | solution.py:26
  77.0 1.2 collective-permute-done.11
  78.7 4.1 %collective-permute-start.12 = (bf16[2,2,128,128]{3,2,1,0:T(8,128)(2,1)S(1)}, bf16[2,2,128,128]{3,2,1,0:T(8,128)(2,1)S(1)}, u32[]{:S(2)}, u32[]{:S(2)}) collective-permute-start(bf16[2,2,128,128]{3,2,1,0:T(8,128)(2,1)S(1)} %copy.53), channel_id=1, source_target_pairs={{0,4},{4,8},{8,12},{12,16},{16,20},{20,24},{24,28},{1,5},{5,9},{9,... | collective-permute-start | bytes 393224 | tf_op jit(solution)/shard_map/ppermute | solution.py:17
  82.8 1.3 collective-permute-start.13
  84.1 2.0 %collective-permute-done.12 = bf16[2,2,128,128]{3,2,1,0:T(8,128)(2,1)S(1)} collective-permute-done((bf16[2,2,128,128]{3,2,1,0:T(8,128)(2,1)S(1)}, bf16[2,2,128,128]{3,2,1,0:T(8,128)(2,1)S(1)}, u32[]{:S(2)}, u32[]{:S(2)}) %collective-permute-start.12) | collective-permute-done | bytes 131104 | tf_op jit(solution)/shard_map/ppermute | solution.py:17
  86.2 3.8 %collective-permute-done.13 = bf16[2,2,128,128]{3,2,1,0:T(8,128)(2,1)S(1)} collective-permute-done((bf16[2,2,128,128]{3,2,1,0:T(8,128)(2,1)S(1)}, bf16[2,2,128,128]{3,2,1,0:T(8,128)(2,1)S(1)}, u32[]{:S(2)}, u32[]{:S(2)}) %collective-permute-start.13) | collective-permute-done | bytes 131104 | tf_op jit(solution)/shard_map/ppermute | solution.py:18
  90.0 2.5 %collective-permute-start.15 = (bf16[2,6,128,128]{3,2,1,0:T(8,128)(2,1)S(1)}, bf16[2,6,128,128]{3,2,1,0:T(8,128)(2,1)S(1)}, u32[]{:S(2)}, u32[]{:S(2)}) collective-permute-start(bf16[2,6,128,128]{3,2,1,0:T(8,128)(2,1)S(1)} %constant_dynamic-update-slice_fusion.3), channel_id=1, source_target_pairs={{1,0},{2,1},{3,2},{5,4},{6,5},{7,6},{9,8},{10,9},{11,10},{13,12},{... | collective-permute-start | bytes 1179656 | tf_op jit(solution)/shard_map/ppermute | solution.py:18
  92.6 3.6 %collective-permute-start.14 = (bf16[2,6,128,128]{3,2,1,0:T(8,128)(2,1)S(1)}, bf16[2,6,128,128]{3,2,1,0:T(8,128)(2,1)S(1)}, u32[]{:S(2)}, u32[]{:S(2)}) collective-permute-start(bf16[2,6,128,128]{3,2,1,0:T(8,128)(2,1)S(1)} %constant_dynamic-update-slice_fusion.3), channel_id=1, source_target_pairs={{0,1},{1,2},{2,3},{4,5},{5,6},{6,7},{8,9},{9,10},{10,11},{12,13},{... | collective-permute-start | bytes 1179656 | tf_op jit(solution)/shard_map/ppermute | solution.py:17
  96.2 3.5 %collective-permute-done.15 = bf16[2,6,128,128]{3,2,1,0:T(8,128)(2,1)S(1)} collective-permute-done((bf16[2,6,128,128]{3,2,1,0:T(8,128)(2,1)S(1)}, bf16[2,6,128,128]{3,2,1,0:T(8,128)(2,1)S(1)}, u32[]{:S(2)}, u32[]{:S(2)}) %collective-permute-start.15) | collective-permute-done | bytes 393248 | tf_op jit(solution)/shard_map/ppermute | solution.py:18
  99.7 1.2 collective-permute-done.14
  101.7 1.1 fusion.2
  103.0 8.4 %all_gather.14 = bf16[8,256,128]{2,1,0:T(8,128)(2,1)S(1)} all-gather(bf16[2,256,128]{2,1,0:T(8,128)(2,1)S(1)} %fusion.18), channel_id=1, replica_groups=mesh['horiz'=8,'vert'=4] {'vert'}, dimensions={0}, use_global_device_ids=true | all-gather | bytes 655360 | tf_op jit(solution)/shard_map/all_gather | solution.py:82
  111.4 1.2 convolution_bitcast_fusion.1
  112.8 2.5 %collective-permute-start.16 = (bf16[256,128]{1,0:T(8,128)(2,1)S(1)}, bf16[256,128]{1,0:T(8,128)(2,1)S(1)}, u32[]{:S(2)}, u32[]{:S(2)}) collective-permute-start(bf16[256,128]{1,0:T(8,128)(2,1)S(1)} %bitcast.96), channel_id=1, source_target_pairs={{0,1},{1,2},{2,3},{4,5},{5,6},{6,7},{8,9},{9,10},{10,11},{12,13},{... | collective-permute-start | bytes 196616 | tf_op jit(solution)/shard_map/ppermute | solution.py:26
  115.4 1.2 collective-permute-done.16
  117.0 3.0 %collective-permute-start.17 = (bf16[2,2,128,128]{3,2,1,0:T(8,128)(2,1)S(1)}, bf16[2,2,128,128]{3,2,1,0:T(8,128)(2,1)S(1)}, u32[]{:S(2)}, u32[]{:S(2)}) collective-permute-start(bf16[2,2,128,128]{3,2,1,0:T(8,128)(2,1)S(1)} %copy.57), channel_id=1, source_target_pairs={{0,4},{4,8},{8,12},{12,16},{16,20},{20,24},{24,28},{1,5},{5,9},{9,... | collective-permute-start | bytes 393224 | tf_op jit(solution)/shard_map/ppermute | solution.py:17
  120.1 1.3 collective-permute-start.18
  121.4 2.0 %collective-permute-done.17 = bf16[2,2,128,128]{3,2,1,0:T(8,128)(2,1)S(1)} collective-permute-done((bf16[2,2,128,128]{3,2,1,0:T(8,128)(2,1)S(1)}, bf16[2,2,128,128]{3,2,1,0:T(8,128)(2,1)S(1)}, u32[]{:S(2)}, u32[]{:S(2)}) %collective-permute-start.17) | collective-permute-done | bytes 131104 | tf_op jit(solution)/shard_map/ppermute | solution.py:17
  123.4 3.8 %collective-permute-done.18 = bf16[2,2,128,128]{3,2,1,0:T(8,128)(2,1)S(1)} collective-permute-done((bf16[2,2,128,128]{3,2,1,0:T(8,128)(2,1)S(1)}, bf16[2,2,128,128]{3,2,1,0:T(8,128)(2,1)S(1)}, u32[]{:S(2)}, u32[]{:S(2)}) %collective-permute-start.18) | collective-permute-done | bytes 131104 | tf_op jit(solution)/shard_map/ppermute | solution.py:18
  127.3 2.5 %collective-permute-start.20 = (bf16[2,6,128,128]{3,2,1,0:T(8,128)(2,1)S(1)}, bf16[2,6,128,128]{3,2,1,0:T(8,128)(2,1)S(1)}, u32[]{:S(2)}, u32[]{:S(2)}) collective-permute-start(bf16[2,6,128,128]{3,2,1,0:T(8,128)(2,1)S(1)} %constant_dynamic-update-slice_fusion.6), channel_id=1, source_target_pairs={{1,0},{2,1},{3,2},{5,4},{6,5},{7,6},{9,8},{10,9},{11,10},{13,12},{... | collective-permute-start | bytes 1179656 | tf_op jit(solution)/shard_map/ppermute | solution.py:18
  129.8 3.8 %collective-permute-start.19 = (bf16[2,6,128,128]{3,2,1,0:T(8,128)(2,1)S(1)}, bf16[2,6,128,128]{3,2,1,0:T(8,128)(2,1)S(1)}, u32[]{:S(2)}, u32[]{:S(2)}) collective-permute-start(bf16[2,6,128,128]{3,2,1,0:T(8,128)(2,1)S(1)} %constant_dynamic-update-slice_fusion.6), channel_id=1, source_target_pairs={{0,1},{1,2},{2,3},{4,5},{5,6},{6,7},{8,9},{9,10},{10,11},{12,13},{... | collective-permute-start | bytes 1179656 | tf_op jit(solution)/shard_map/ppermute | solution.py:17
  133.6 3.3 %collective-permute-done.20 = bf16[2,6,128,128]{3,2,1,0:T(8,128)(2,1)S(1)} collective-permute-done((bf16[2,6,128,128]{3,2,1,0:T(8,128)(2,1)S(1)}, bf16[2,6,128,128]{3,2,1,0:T(8,128)(2,1)S(1)}, u32[]{:S(2)}, u32[]{:S(2)}) %collective-permute-start.20) | collective-permute-done | bytes 393248 | tf_op jit(solution)/shard_map/ppermute | solution.py:18
  137.0 1.2 collective-permute-done.19
  139.0 1.2 fusion
  140.3 8.4 %all_gather.15 = bf16[8,256,128]{2,1,0:T(8,128)(2,1)S(1)} all-gather(bf16[2,256,128]{2,1,0:T(8,128)(2,1)S(1)} %fusion.19), channel_id=1, replica_groups=mesh['horiz'=8,'vert'=4] {'vert'}, dimensions={0}, use_global_device_ids=true | all-gather | bytes 655360 | tf_op jit(solution)/shard_map/all_gather | solution.py:82
  148.7 1.2 convolution_bitcast_fusion
  150.0 2.5 %collective-permute-start.21 = (bf16[256,128]{1,0:T(8,128)(2,1)S(1)}, bf16[256,128]{1,0:T(8,128)(2,1)S(1)}, u32[]{:S(2)}, u32[]{:S(2)}) collective-permute-start(bf16[256,128]{1,0:T(8,128)(2,1)S(1)} %bitcast.97), channel_id=1, source_target_pairs={{0,1},{1,2},{2,3},{4,5},{5,6},{6,7},{8,9},{9,10},{10,11},{12,13},{... | collective-permute-start | bytes 196616 | tf_op jit(solution)/shard_map/ppermute | solution.py:26
  152.6 1.2 collective-permute-done.21
  (77 shorter events, 16.1 us)
Async XLA Ops:
  0.0 25.5 %copy-start = (bf16[2,2,7,128,128]{4,3,2,1,0:T(8,128)(2,1)S(1)}, bf16[2,2,7,128,128]{4,3,2,1,0:T(8,128)(2,1)}, u32[]{:S(2)}) copy-start(bf16[2,2,7,128,128]{4,3,2,1,0:T(8,128)(2,1)} %param.9) | copy-start | bytes 2752516
  0.0 23.6 %copy-start.1 = (bf16[2,256,128]{2,1,0:T(8,128)(2,1)S(1)}, bf16[2,256,128]{2,1,0:T(8,128)(2,1)}, u32[]{:S(2)}) copy-start(bf16[2,256,128]{2,1,0:T(8,128)(2,1)} %param.8) | copy-start | bytes 393220
  0.0 23.3 %copy-start.2 = (f32[64,8,8]{0,2,1:T(8,128)S(1)}, f32[64,8,8]{0,2,1:T(8,128)}, u32[]{:S(2)}) copy-start(f32[64,8,8]{0,2,1:T(8,128)} %param.13) | copy-start | bytes 49156
  0.0 9.3 %collective-permute-start.1 = (bf16[2,2,128,128]{3,2,1,0:T(8,128)(2,1)}, bf16[2,2,128,128]{3,2,1,0:T(8,128)(2,1)S(1)}, u32[]{:S(2)}, u32[]{:S(2)}) collective-permute-start(bf16[2,2,128,128]{3,2,1,0:T(8,128)(2,1)} %bitcast.86), channel_id=1, source_target_pairs={{4,0},{8,4},{12,8},{16,12},{20,16},{24,20},{28,24},{5,1},{9,5},{13... | collective-permute-start | bytes 393224 | tf_op jit(solution)/shard_map/ppermute | solution.py:18
  1.4 9.9 %collective-permute-start = (bf16[2,2,128,128]{3,2,1,0:T(8,128)(2,1)}, bf16[2,2,128,128]{3,2,1,0:T(8,128)(2,1)S(1)}, u32[]{:S(2)}, u32[]{:S(2)}) collective-permute-start(bf16[2,2,128,128]{3,2,1,0:T(8,128)(2,1)} %bitcast.87), channel_id=1, source_target_pairs={{0,4},{4,8},{8,12},{12,16},{16,20},{20,24},{24,28},{1,5},{5,9},{9,... | collective-permute-start | bytes 393224 | tf_op jit(solution)/shard_map/ppermute | solution.py:17
  6.1 11.8 %collective-permute-start.4 = (f32[64,8,8]{0,2,1:T(8,128)}, f32[64,8,8]{0,2,1:T(8,128)S(1)}, u32[]{:S(2)}, u32[]{:S(2)}) collective-permute-start(f32[64,8,8]{0,2,1:T(8,128)} %param.13), channel_id=1, source_target_pairs={{0,3},{1,0},{2,1},{3,2},{4,7},{5,4},{6,5},{7,6},{8,11},{9,8},{10,9... | collective-permute-start | bytes 49160 | tf_op jit(solution)/shard_map/ppermute | solution.py:61
  9.3 16.7 %copy-start.4 = (bf16[2,2,7]{2,1,0:T(2,128)(2,1)}, bf16[2,2,7]{2,1,0:T(2,128)(2,1)S(1)}, u32[]{:S(2)}) copy-start(bf16[2,2,7]{2,1,0:T(2,128)(2,1)S(1)} %compare_convert_fusion) | copy-start | bytes 172
  12.3 11.3 %collective-permute-start.3 = (bf16[2,6,128,128]{3,2,1,0:T(8,128)(2,1)S(1)}, bf16[2,6,128,128]{3,2,1,0:T(8,128)(2,1)S(1)}, u32[]{:S(2)}, u32[]{:S(2)}) collective-permute-start(bf16[2,6,128,128]{3,2,1,0:T(8,128)(2,1)S(1)} %pad_maximum_fusion.4), channel_id=1, source_target_pairs={{1,0},{2,1},{3,2},{5,4},{6,5},{7,6},{9,8},{10,9},{11,10},{13,12},{... | collective-permute-start | bytes 1179656 | tf_op jit(solution)/shard_map/ppermute | solution.py:18
  14.7 8.9 %collective-permute-start.2 = (bf16[2,6,128,128]{3,2,1,0:T(8,128)(2,1)S(1)}, bf16[2,6,128,128]{3,2,1,0:T(8,128)(2,1)}, u32[]{:S(2)}, u32[]{:S(2)}) collective-permute-start(bf16[2,6,128,128]{3,2,1,0:T(8,128)(2,1)S(1)} %pad_maximum_fusion.4), channel_id=1, source_target_pairs={{0,1},{1,2},{2,3},{4,5},{5,6},{6,7},{8,9},{9,10},{10,11},{12,13},{... | collective-permute-start | bytes 1179656 | tf_op jit(solution)/shard_map/ppermute | solution.py:17
  18.7 4.5 %collective-permute-start.5 = (f32[128,8,8]{0,2,1:T(8,128)S(1)}, f32[128,8,8]{0,2,1:T(8,128)S(1)}, u32[]{:S(2)}, u32[]{:S(2)}) collective-permute-start(f32[128,8,8]{0,2,1:T(8,128)S(1)} %pad_maximum_fusion.5), channel_id=1, source_target_pairs={{0,2},{1,3},{2,0},{3,1},{4,6},{5,7},{6,4},{7,5},{8,10},{9,11},{10,... | collective-permute-start | bytes 98312 | tf_op jit(solution)/shard_map/ppermute | solution.py:61
  26.1 12.6 %copy-start.3 = (f32[128]{0:T(128)S(1)}, f32[128]{0:T(128)}, u32[]{:S(2)}) copy-start(f32[128]{0:T(128)} %param.14) | copy-start | bytes 1540
  35.3 4.7 %collective-permute-start.6 = (bf16[256,128]{1,0:T(8,128)(2,1)S(1)}, bf16[256,128]{1,0:T(8,128)(2,1)S(1)}, u32[]{:S(2)}, u32[]{:S(2)}) collective-permute-start(bf16[256,128]{1,0:T(8,128)(2,1)S(1)} %bitcast.94), channel_id=1, source_target_pairs={{0,1},{1,2},{2,3},{4,5},{5,6},{6,7},{8,9},{9,10},{10,11},{12,13},{... | collective-permute-start | bytes 196616 | tf_op jit(solution)/shard_map/ppermute | solution.py:26
  40.4 6.3 %collective-permute-start.7 = (bf16[2,2,128,128]{3,2,1,0:T(8,128)(2,1)S(1)}, bf16[2,2,128,128]{3,2,1,0:T(8,128)(2,1)S(1)}, u32[]{:S(2)}, u32[]{:S(2)}) collective-permute-start(bf16[2,2,128,128]{3,2,1,0:T(8,128)(2,1)S(1)} %copy.48), channel_id=1, source_target_pairs={{0,4},{4,8},{8,12},{12,16},{16,20},{20,24},{24,28},{1,5},{5,9},{9,... | collective-permute-start | bytes 393224 | tf_op jit(solution)/shard_map/ppermute | solution.py:17
  44.5 6.4 %collective-permute-start.8 = (bf16[2,2,128,128]{3,2,1,0:T(8,128)(2,1)S(1)}, bf16[2,2,128,128]{3,2,1,0:T(8,128)(2,1)S(1)}, u32[]{:S(2)}, u32[]{:S(2)}) collective-permute-start(bf16[2,2,128,128]{3,2,1,0:T(8,128)(2,1)S(1)} %copy.48), channel_id=1, source_target_pairs={{4,0},{8,4},{12,8},{16,12},{20,16},{24,20},{28,24},{5,1},{9,5},{13... | collective-permute-start | bytes 393224 | tf_op jit(solution)/shard_map/ppermute | solution.py:18
  50.9 10.4 %collective-permute-start.10 = (bf16[2,6,128,128]{3,2,1,0:T(8,128)(2,1)S(1)}, bf16[2,6,128,128]{3,2,1,0:T(8,128)(2,1)S(1)}, u32[]{:S(2)}, u32[]{:S(2)}) collective-permute-start(bf16[2,6,128,128]{3,2,1,0:T(8,128)(2,1)S(1)} %constant_dynamic-update-slice_fusion), channel_id=1, source_target_pairs={{1,0},{2,1},{3,2},{5,4},{6,5},{7,6},{9,8},{10,9},{11,10},{13,12},{... | collective-permute-start | bytes 1179656 | tf_op jit(solution)/shard_map/ppermute | solution.py:18
  52.9 9.7 %collective-permute-start.9 = (bf16[2,6,128,128]{3,2,1,0:T(8,128)(2,1)S(1)}, bf16[2,6,128,128]{3,2,1,0:T(8,128)(2,1)S(1)}, u32[]{:S(2)}, u32[]{:S(2)}) collective-permute-start(bf16[2,6,128,128]{3,2,1,0:T(8,128)(2,1)S(1)} %constant_dynamic-update-slice_fusion), channel_id=1, source_target_pairs={{0,1},{1,2},{2,3},{4,5},{5,6},{6,7},{8,9},{9,10},{10,11},{12,13},{... | collective-permute-start | bytes 1179656 | tf_op jit(solution)/shard_map/ppermute | solution.py:17
  74.4 3.8 %collective-permute-start.11 = (bf16[256,128]{1,0:T(8,128)(2,1)S(1)}, bf16[256,128]{1,0:T(8,128)(2,1)S(1)}, u32[]{:S(2)}, u32[]{:S(2)}) collective-permute-start(bf16[256,128]{1,0:T(8,128)(2,1)S(1)} %bitcast.95), channel_id=1, source_target_pairs={{0,1},{1,2},{2,3},{4,5},{5,6},{6,7},{8,9},{9,10},{10,11},{12,13},{... | collective-permute-start | bytes 196616 | tf_op jit(solution)/shard_map/ppermute | solution.py:26
  78.7 7.4 %collective-permute-start.12 = (bf16[2,2,128,128]{3,2,1,0:T(8,128)(2,1)S(1)}, bf16[2,2,128,128]{3,2,1,0:T(8,128)(2,1)S(1)}, u32[]{:S(2)}, u32[]{:S(2)}) collective-permute-start(bf16[2,2,128,128]{3,2,1,0:T(8,128)(2,1)S(1)} %copy.53), channel_id=1, source_target_pairs={{0,4},{4,8},{8,12},{12,16},{16,20},{20,24},{24,28},{1,5},{5,9},{9,... | collective-permute-start | bytes 393224 | tf_op jit(solution)/shard_map/ppermute | solution.py:17
  82.8 7.2 %collective-permute-start.13 = (bf16[2,2,128,128]{3,2,1,0:T(8,128)(2,1)S(1)}, bf16[2,2,128,128]{3,2,1,0:T(8,128)(2,1)S(1)}, u32[]{:S(2)}, u32[]{:S(2)}) collective-permute-start(bf16[2,2,128,128]{3,2,1,0:T(8,128)(2,1)S(1)} %copy.53), channel_id=1, source_target_pairs={{4,0},{8,4},{12,8},{16,12},{20,16},{24,20},{28,24},{5,1},{9,5},{13... | collective-permute-start | bytes 393224 | tf_op jit(solution)/shard_map/ppermute | solution.py:18
  90.0 9.7 %collective-permute-start.15 = (bf16[2,6,128,128]{3,2,1,0:T(8,128)(2,1)S(1)}, bf16[2,6,128,128]{3,2,1,0:T(8,128)(2,1)S(1)}, u32[]{:S(2)}, u32[]{:S(2)}) collective-permute-start(bf16[2,6,128,128]{3,2,1,0:T(8,128)(2,1)S(1)} %constant_dynamic-update-slice_fusion.3), channel_id=1, source_target_pairs={{1,0},{2,1},{3,2},{5,4},{6,5},{7,6},{9,8},{10,9},{11,10},{13,12},{... | collective-permute-start | bytes 1179656 | tf_op jit(solution)/shard_map/ppermute | solution.py:18
  92.6 8.3 %collective-permute-start.14 = (bf16[2,6,128,128]{3,2,1,0:T(8,128)(2,1)S(1)}, bf16[2,6,128,128]{3,2,1,0:T(8,128)(2,1)S(1)}, u32[]{:S(2)}, u32[]{:S(2)}) collective-permute-start(bf16[2,6,128,128]{3,2,1,0:T(8,128)(2,1)S(1)} %constant_dynamic-update-slice_fusion.3), channel_id=1, source_target_pairs={{0,1},{1,2},{2,3},{4,5},{5,6},{6,7},{8,9},{9,10},{10,11},{12,13},{... | collective-permute-start | bytes 1179656 | tf_op jit(solution)/shard_map/ppermute | solution.py:17
  112.8 3.8 %collective-permute-start.16 = (bf16[256,128]{1,0:T(8,128)(2,1)S(1)}, bf16[256,128]{1,0:T(8,128)(2,1)S(1)}, u32[]{:S(2)}, u32[]{:S(2)}) collective-permute-start(bf16[256,128]{1,0:T(8,128)(2,1)S(1)} %bitcast.96), channel_id=1, source_target_pairs={{0,1},{1,2},{2,3},{4,5},{5,6},{6,7},{8,9},{9,10},{10,11},{12,13},{... | collective-permute-start | bytes 196616 | tf_op jit(solution)/shard_map/ppermute | solution.py:26
  117.0 6.3 %collective-permute-start.17 = (bf16[2,2,128,128]{3,2,1,0:T(8,128)(2,1)S(1)}, bf16[2,2,128,128]{3,2,1,0:T(8,128)(2,1)S(1)}, u32[]{:S(2)}, u32[]{:S(2)}) collective-permute-start(bf16[2,2,128,128]{3,2,1,0:T(8,128)(2,1)S(1)} %copy.57), channel_id=1, source_target_pairs={{0,4},{4,8},{8,12},{12,16},{16,20},{20,24},{24,28},{1,5},{5,9},{9,... | collective-permute-start | bytes 393224 | tf_op jit(solution)/shard_map/ppermute | solution.py:17
  120.1 7.2 %collective-permute-start.18 = (bf16[2,2,128,128]{3,2,1,0:T(8,128)(2,1)S(1)}, bf16[2,2,128,128]{3,2,1,0:T(8,128)(2,1)S(1)}, u32[]{:S(2)}, u32[]{:S(2)}) collective-permute-start(bf16[2,2,128,128]{3,2,1,0:T(8,128)(2,1)S(1)} %copy.57), channel_id=1, source_target_pairs={{4,0},{8,4},{12,8},{16,12},{20,16},{24,20},{28,24},{5,1},{9,5},{13... | collective-permute-start | bytes 393224 | tf_op jit(solution)/shard_map/ppermute | solution.py:18
  127.3 9.7 %collective-permute-start.20 = (bf16[2,6,128,128]{3,2,1,0:T(8,128)(2,1)S(1)}, bf16[2,6,128,128]{3,2,1,0:T(8,128)(2,1)S(1)}, u32[]{:S(2)}, u32[]{:S(2)}) collective-permute-start(bf16[2,6,128,128]{3,2,1,0:T(8,128)(2,1)S(1)} %constant_dynamic-update-slice_fusion.6), channel_id=1, source_target_pairs={{1,0},{2,1},{3,2},{5,4},{6,5},{7,6},{9,8},{10,9},{11,10},{13,12},{... | collective-permute-start | bytes 1179656 | tf_op jit(solution)/shard_map/ppermute | solution.py:18
  129.8 8.3 %collective-permute-start.19 = (bf16[2,6,128,128]{3,2,1,0:T(8,128)(2,1)S(1)}, bf16[2,6,128,128]{3,2,1,0:T(8,128)(2,1)S(1)}, u32[]{:S(2)}, u32[]{:S(2)}) collective-permute-start(bf16[2,6,128,128]{3,2,1,0:T(8,128)(2,1)S(1)} %constant_dynamic-update-slice_fusion.6), channel_id=1, source_target_pairs={{0,1},{1,2},{2,3},{4,5},{5,6},{6,7},{8,9},{9,10},{10,11},{12,13},{... | collective-permute-start | bytes 1179656 | tf_op jit(solution)/shard_map/ppermute | solution.py:17
  150.0 3.8 %collective-permute-start.21 = (bf16[256,128]{1,0:T(8,128)(2,1)S(1)}, bf16[256,128]{1,0:T(8,128)(2,1)S(1)}, u32[]{:S(2)}, u32[]{:S(2)}) collective-permute-start(bf16[256,128]{1,0:T(8,128)(2,1)S(1)} %bitcast.97), channel_id=1, source_target_pairs={{0,1},{1,2},{2,3},{4,5},{5,6},{6,7},{8,9},{9,10},{10,11},{12,13},{... | collective-permute-start | bytes 196616 | tf_op jit(solution)/shard_map/ppermute | solution.py:26
